TPU v7x, 128 devices: a whole 4x4x4 slice. The times are simulated.
128 devices in a mesh: row: 16 (over x, y_hi, core), col: 8 (over y_lo, z).
Axes of the slice: x: 4, y: 4 (y_hi: 2, y_lo: 2; y = y_hi * 2 + y_lo), z: 4, core: 2. Of those that a mesh axis runs over, the one named last changes fastest.
Arguments:
- inputs: bfloat16 [1024, 8192], P('col', 'row'), may hold values from -6 to 6
- cotangent: bfloat16 [1024, 8192], P('col', 'row'), may hold values from -1.5 to 1.5
- gate_weight: bfloat16 [8192, 14336], P('row', 'col'), may hold values from -0.0625 to 0.0625
- up_weight: bfloat16 [8192, 14336], P('row', 'col'), may hold values from -0.0625 to 0.0625
- down_weight: bfloat16 [14336, 8192], P('col', 'row'), may hold values from -0.046875 to 0.046875
Outputs:
- grad_inputs: bfloat16 [1024, 8192], P('col', 'row')
- grad_gate: bfloat16 [8192, 14336], P('row', 'col')
- grad_up: bfloat16 [8192, 14336], P('row', 'col')
- grad_down: bfloat16 [14336, 8192], P('col', 'row')
All inputs are finite; a program needn't handle non-finite values.
Results may differ from a plain program's by a relative error of at most 0.015.
Values may be sent and summed in bfloat16 or wider, within the bound.
A program may use at most 128 MiB of HBM per device.

v0:
```python
import jax
import jax.numpy as jnp
from jax import lax
from jax.sharding import PartitionSpec as P


def reduce_rows(panel, product, stacked, columns, share_rows):
    return lax.psum_scatter(
        product(panel).reshape(lax.axis_size("row") * share_rows, stacked, columns),
        "row",
        scatter_dimension=0,
        tiled=True,
    )


def collect(pieces):
    return lax.all_gather(pieces, "row", axis=0, tiled=True)


def hidden_of(gate_up):
    gate_val = gate_up[:, 0:1].astype(jnp.float32)
    up_val = gate_up[:, 1:2].astype(jnp.float32)
    return (gate_val * jax.nn.sigmoid(gate_val) * up_val).astype(jnp.bfloat16)


def grads_of(gate_up, hidden_grad):
    gate_val = gate_up[:, 0:1].astype(jnp.float32)
    up_val = gate_up[:, 1:2].astype(jnp.float32)
    grad_val = hidden_grad.astype(jnp.float32)
    sigmoid_gate = jax.nn.sigmoid(gate_val)
    gate_grad = (grad_val * up_val * sigmoid_gate * (1.0 + gate_val * (1.0 - sigmoid_gate))).astype(
        jnp.bfloat16
    )
    up_grad = (grad_val * gate_val * sigmoid_gate).astype(jnp.bfloat16)
    return jnp.concatenate([gate_grad, up_grad], axis=1)


def on_device(inputs, cotangent, gate_weight, up_weight, down_weight):
    columns = gate_weight.shape[1]
    weights_pair = jnp.concatenate([gate_weight, up_weight], axis=1)
    inputs_all, cotangent_all = (
        lax.all_gather(inputs, "col", axis=0, tiled=True),
        lax.all_gather(cotangent, "col", axis=0, tiled=True),
    )
    tokens_all = inputs_all.shape[0]
    share_rows = tokens_all // lax.axis_size("row")

    def forward_term(rows_block):
        return jnp.dot(rows_block, weights_pair, preferred_element_type=jnp.float32)

    def backward_term(rows_block):
        return lax.dot_general(
            rows_block, down_weight, (((1,), (1,)), ((), ())), preferred_element_type=jnp.float32
        )

    gate_up = reduce_rows(inputs_all, forward_term, 2, columns, share_rows).astype(jnp.bfloat16)
    hidden_all = collect(hidden_of(gate_up))
    hidden_grad = reduce_rows(cotangent_all, backward_term, 1, columns, share_rows).astype(
        jnp.bfloat16
    )
    pair_all = collect(grads_of(gate_up, hidden_grad))
    hidden_flat = hidden_all.reshape(tokens_all, columns)
    pair_flat = pair_all.reshape(tokens_all, 2 * columns)
    grad_down = lax.dot_general(
        hidden_flat, cotangent_all, (((0,), (0,)), ((), ())), preferred_element_type=jnp.float32
    ).astype(jnp.bfloat16)
    grad_pair = lax.dot_general(
        inputs_all, pair_flat, (((0,), (0,)), ((), ())), preferred_element_type=jnp.float32
    )
    grad_gate = grad_pair[:, :columns].astype(jnp.bfloat16)
    grad_up = grad_pair[:, columns:].astype(jnp.bfloat16)
    rows_block = pair_flat
    grad_inputs = lax.psum_scatter(
        lax.dot_general(
            rows_block, weights_pair, (((1,), (1,)), ((), ())), preferred_element_type=jnp.float32
        ),
        "col",
        scatter_dimension=0,
        tiled=True,
    ).astype(jnp.bfloat16)
    return (grad_inputs, grad_gate, grad_up, grad_down)


def solution(mesh):
    placed = (P("col", "row"), P("col", "row"), P("row", "col"), P("row", "col"), P("col", "row"))
    return jax.shard_map(
        on_device,
        mesh=mesh,
        in_specs=placed,
        out_specs=(P("col", "row"), P("row", "col"), P("row", "col"), P("col", "row")),
        check_vma=False,
    )
```

profile of v0, /device:TPU:1, one launch (start us, length us, event | category | flops | bytes accessed | tf_op | source)
XLA Modules:
  0.0 497.2 jit_solution(12590982803068620551)
XLA Ops:
  7.2 0.0 copy-start
  7.2 0.0 all-gather.7.cloned.1.call-start
  7.2 0.7 all-gather.7.cloned.1.call-update
  7.9 0.0 all-gather.5.cloned.1.call-start
  8.0 0.7 all-gather.5.cloned.1.call-update
  8.7 0.0 reduce-scatter.6.cloned.1.call-start
  8.7 0.0 copy-start.2
  8.7 3.0 constant_dynamic-update-slice_fusion.1
  11.7 0.0 copy-done.2
  11.8 1.4 constant_dynamic-update-slice_fusion
  13.2 34.1 %all-gather.7.cloned.1.call-done = bf16[1024,512]{1,0:T(8,128)(2,1)} async-done(((bf16[128,512]{1,0:T(8,128)(2,1)}), bf16[1024,512]{1,0:T(8,128)(2,1)}) %all-gather.7.cloned.1.call-update) | async-done | bytes 1048592 | tf_op jit(solution)/shard_map/all_gather | solution.py:42
  47.3 11.5 %fusion.17 = f32[3584,1024]{1,0:T(8,128)} fusion(bf16[512,3584]{1,0:T(8,128)(2,1)} %constant_dynamic-update-slice_fusion, bf16[1024,512]{1,0:T(8,128)(2,1)} %all-gather.7.cloned.1.call-done), kind=kOutput, calls=%fused_computation.26 | convolution fusion | flops 3758096384 | bytes 19398656 | tf_op jit(solution)/shard_map/dot_general | solution.py:49
  58.8 14.4 %copy.11 = f32[1024,2,1792]{2,0,1:T(8,128)} copy(f32[1024,2,1792]{0,2,1:T(8,128)} %bitcast.22) | data formatting | bytes 29360128 | tf_op jit(solution)/shard_map/reshape | solution.py:9
  73.2 0.0 reduce-scatter.6.cloned.1.call-update
  73.2 0.0 reduce-scatter.4.cloned.1.call-start
  73.3 13.9 %all-gather.5.cloned.1.call-done = bf16[1024,512]{1,0:T(8,128)(2,1)} async-done(((bf16[128,512]{1,0:T(8,128)(2,1)}), bf16[1024,512]{1,0:T(8,128)(2,1)}) %all-gather.5.cloned.1.call-update) | async-done | bytes 1048592 | tf_op jit(solution)/shard_map/all_gather | solution.py:43
  87.2 0.0 copy-done
  87.2 6.3 %convolution_bitcast_fusion = f32[1024,1,1792]{2,0,1:T(8,128)} fusion(bf16[1024,512]{1,0:T(8,128)(2,1)} %all-gather.5.cloned.1.call-done, bf16[1792,512]{1,0:T(8,128)(2,1)S(1)} %copy-done), kind=kOutput, calls=%fused_computation.2 | convolution fusion | flops 1879048192 | bytes 10223616 | tf_op jit(solution)/shard_map/dot_general | solution.py:52
  93.4 0.0 reduce-scatter.4.cloned.1.call-update
  93.5 0.0 all-gather.9.cloned.1.call-start
  93.5 133.7 %reduce-scatter.6.cloned.1.call-done = f32[64,2,1792]{2,0,1:T(8,128)} async-done(((f32[1024,2,1792]{2,0,1:T(8,128)}), f32[64,2,1792]{2,0,1:T(8,128)}) %reduce-scatter.6.cloned.1.call-update) | async-done | bytes 917520 | tf_op jit(solution)/shard_map/reduce_scatter | solution.py:8
  227.2 1.2 convert_element_type.36
  228.4 94.9 %reduce-scatter.4.cloned.1.call-done = f32[64,1,1792]{2,0,1:T(8,128)} async-done(((f32[1024,1,1792]{2,0,1:T(8,128)}), f32[64,1,1792]{2,0,1:T(8,128)}) %reduce-scatter.4.cloned.1.call-update) | async-done | bytes 458768 | tf_op jit(solution)/shard_map/reduce_scatter | solution.py:8
  323.3 2.0 fusion.8
  325.3 0.8 pad_maximum_fusion
  326.1 0.0 all-gather.9.cloned.1.call-update
  326.1 0.0 all-gather.11.cloned.1.call-start
  326.2 0.5 all-gather.11.cloned.1.call-update
  326.7 0.2 reduce-scatter.8.cloned.1.call-start
  326.9 68.5 %all-gather.9.cloned.1.call-done = bf16[1024,2,1792]{2,0,1:T(8,128)(2,1)} async-done(((bf16[64,2,1792]{2,0,1:T(8,128)(2,1)}), bf16[1024,2,1792]{2,0,1:T(8,128)(2,1)}) %all-gather.9.cloned.1.call-update) | async-done | bytes 7340048 | tf_op jit(solution)/shard_map/all_gather | solution.py:17
  395.5 9.9 %copy.12 = bf16[1024,2,1792]{0,2,1:T(8,128)(2,1)} copy(bf16[1024,2,1792]{2,0,1:T(8,128)(2,1)} %all-gather.9.cloned.1.call-done) | data formatting | bytes 14680064 | tf_op jit(solution)/shard_map/all_gather | solution.py:17
  405.4 0.0 copy-start.4
  405.4 9.7 %fusion.18 = f32[1024,512]{1,0:T(8,128)} fusion(bf16[1024,3584]{0,1:T(8,128)(2,1)} %bitcast.23, bf16[512,3584]{1,0:T(8,128)(2,1)} %constant_dynamic-update-slice_fusion), kind=kOutput, calls=%fused_computation.27 | convolution fusion | flops 3758096384 | bytes 13107200 | tf_op jit(solution)/shard_map/dot_general | solution.py:74
  415.1 0.0 reduce-scatter.8.cloned.1.call-update
  415.1 0.0 copy-start.3
  415.2 35.2 %all-gather.11.cloned.1.call-done = bf16[1024,1,1792]{2,0,1:T(8,128)(2,1)} async-done(((bf16[64,1,1792]{2,0,1:T(8,128)(2,1)}), bf16[1024,1,1792]{2,0,1:T(8,128)(2,1)}) %all-gather.11.cloned.1.call-update) | async-done | bytes 3670032 | tf_op jit(solution)/shard_map/all_gather | solution.py:17
  450.4 0.0 copy-done.4
  450.4 5.4 %fusion.3 = bf16[1792,512]{1,0:T(8,128)(2,1)} fusion(bf16[1024,512]{1,0:T(8,128)(2,1)S(1)} %copy-done.4, bf16[1024,1,1792]{2,0,1:T(8,128)(2,1)} %all-gather.11.cloned.1.call-done), kind=kOutput, calls=%fused_computation.5 | convolution fusion | flops 1879965696 | bytes 6553600 | tf_op jit(solution)/shard_map/dot_general | solution.py:64
  455.7 0.0 copy-done.3
  455.7 7.3 %fusion = bf16[512,3584]{0,1:T(8,128)(2,1)S(1)} fusion(bf16[1024,3584]{0,1:T(8,128)(2,1)} %bitcast.24, bf16[1024,512]{1,0:T(8,128)(2,1)S(1)} %copy-done.3), kind=kOutput, calls=%fused_computation.1 | convolution fusion | flops 3759931392 | bytes 12058624 | tf_op jit(solution)/shard_map/dot_general | solution.py:67
  463.0 2.1 fusion.16
  465.1 0.0 copy-start.1
  465.1 3.9 copy.13
  469.0 3.8 copy.14
  472.8 15.9 %reduce-scatter.8.cloned.1.call-done = f32[128,512]{1,0:T(8,128)} async-done(((f32[1024,512]{1,0:T(8,128)}), f32[128,512]{1,0:T(8,128)}) %reduce-scatter.8.cloned.1.call-update) | async-done | bytes 262160 | tf_op jit(solution)/shard_map/reduce_scatter | solution.py:73
  488.7 1.6 convert_element_type.41
  490.3 0.0 copy-done.1
Async XLA Ops:
  7.2 80.0 %copy-start = (bf16[1792,512]{1,0:T(8,128)(2,1)S(1)}, bf16[1792,512]{1,0:T(8,128)(2,1)}, u32[]{:S(2)}) copy-start(bf16[1792,512]{1,0:T(8,128)(2,1)} %param.9) | copy-start | bytes 5505028
  7.2 40.1 %all-gather.7.cloned.1.call-start = ((), (), s32[]{:S(2)}) async-start(), calls=%async_computation.5 | async-start | bytes 1179648 | tf_op jit(solution)/shard_map/all_gather | solution.py:42
  7.9 79.2 %all-gather.5.cloned.1.call-start = ((), (), s32[]{:S(2)}) async-start(), calls=%async_computation.3 | async-start | bytes 1179648 | tf_op jit(solution)/shard_map/all_gather | solution.py:43
  8.7 218.5 %reduce-scatter.6.cloned.1.call-start = ((), (), s32[]{:S(2)}) async-start(), calls=%async_computation.6 | async-start | bytes 15597568 | tf_op jit(solution)/shard_map/reduce_scatter | solution.py:8
  8.7 3.0 copy-start.2
  73.2 250.1 %reduce-scatter.4.cloned.1.call-start = ((), (), s32[]{:S(2)}) async-start(), calls=%async_computation.4 | async-start | bytes 7798784 | tf_op jit(solution)/shard_map/reduce_scatter | solution.py:8
  93.5 302.0 %all-gather.9.cloned.1.call-start = ((), (), s32[]{:S(2)}) async-start(), calls=%async_computation.7 | async-start | bytes 7798784 | tf_op jit(solution)/shard_map/all_gather | solution.py:17
  326.1 124.2 %all-gather.11.cloned.1.call-start = ((), (), s32[]{:S(2)}) async-start(), calls=%async_computation.9 | async-start | bytes 3899392 | tf_op jit(solution)/shard_map/all_gather | solution.py:17
  326.7 162.0 %reduce-scatter.8.cloned.1.call-start = ((), (), s32[]{:S(2)}) async-start(), calls=%async_computation.8 | async-start | bytes 2359296 | tf_op jit(solution)/shard_map/reduce_scatter | solution.py:73
  405.4 45.0 %copy-start.4 = (bf16[1024,512]{1,0:T(8,128)(2,1)S(1)}, bf16[1024,512]{1,0:T(8,128)(2,1)}, u32[]{:S(2)}) copy-start(bf16[1024,512]{1,0:T(8,128)(2,1)} %all-gather.5.cloned.1.call-done) | copy-start | bytes 3145732
  415.1 40.6 %copy-start.3 = (bf16[1024,512]{1,0:T(8,128)(2,1)S(1)}, bf16[1024,512]{1,0:T(8,128)(2,1)}, u32[]{:S(2)}) copy-start(bf16[1024,512]{1,0:T(8,128)(2,1)} %all-gather.7.cloned.1.call-done) | copy-start | bytes 3145732
  465.1 25.3 %copy-start.1 = (bf16[1792,512]{1,0:T(8,128)(2,1)S(1)}, bf16[1792,512]{1,0:T(8,128)(2,1)}, u32[]{:S(2)}) copy-start(bf16[1792,512]{1,0:T(8,128)(2,1)} %param.9) | copy-start | bytes 5505028
Sparse Core Ops, SparseCore 0:
  9.7 37.5 all-gather.6
  48.9 38.1 all-gather.4
  91.5 135.5 reduce-scatter.5
  231.8 91.4 reduce-scatter.3
  326.2 69.1 all-gather.8
  398.3 52.0 all-gather.10
  452.8 35.9 reduce-scatter.7
where the time goes:
time: 502 us; the launch traced here: 497 us
  waiting for transfers between devices  398 us (79%)
  matrix products  40.1 us (8%)
  local copies, waits for them, and re-layouts  38.6 us (8%)
  between operations  14.2 us (3%)
  other arithmetic  5.64 us (1%)
    reduce_scatter x2, waiting for transfers between devices, reduce_rows(): lax.psum_scatter(product(panel).reshape(lax.axis_size('row') * share_rows...  229 us
    all_gather x2, waiting for transfers between devices, collect(): return lax.all_gather(pieces, 'row', axis=0, tiled=True)  104 us
    all_gather x1, waiting for transfers between devices, on_device(): lax.all_gather(inputs, 'col', axis=0, tiled=True)  34.1 us
    reduce_scatter x1, waiting for transfers between devices, on_device(): lax.psum_scatter(lax.dot_general(rows_block, weights_pair, (((1,), (1,)),...  15.9 us
    reshape x1, local copies, waits for them, and re-layouts, reduce_rows(): product(panel).reshape(lax.axis_size('row') * share_rows, stacked, columns)  14.4 us
    all_gather x1, waiting for transfers between devices, on_device(): lax.all_gather(cotangent, 'col', axis=0, tiled=True)  13.9 us
    dot_general x1, matrix products, forward_term(): return jnp.dot(rows_block, weights_pair, preferred_element_type=jnp.float32)  11.5 us
    unnamed x13, local copies, waits for them, and re-layouts  10.8 us
  transfers between devices with their start and end apart: 7, of which 7 were waited for; matrix products, arithmetic and copies ran while one was open for 16% of the time, Pallas kernels for 0%

commit v1 on v0

v1 whole, which is shorter than its diff:
```python
import jax
import jax.numpy as jnp
from jax import lax
from jax.experimental import pallas as pl
from jax.experimental.pallas import tpu as pltpu
from jax.sharding import PartitionSpec as P

MESH = pl.DeviceIdType.MESH
BLOCKS = 8
STEPS = 8
CORE, FIRST, SECOND, FAR, FAR_BACK, SECOND_BACK, FIRST_BACK, CORE_BACK = range(STEPS)
NT = (((1,), (1,)), ((), ()))
TN = (((0,), (0,)), ((), ()))


def dot(a, b, dims=(((1,), (0,)), ((), ()))):
    return lax.dot_general(a, b, dims, preferred_element_type=jnp.float32)


def kernel(
    x_in, y_in, gate_in, up_in, down_in,
    gx_out, gg_out, gu_out, gd_out,
    xs, ys, wg, wu, wd, part, r_core, r_first, r_second, r_far, full, acc_gate, acc_up, acc_down,
    dx_send, dx_recv, dx_out, local_sem, send_sem, recv_sem, col_send, col_recv, dx_ssem, dx_rsem,
):
    rows = x_in.shape[0]
    width = x_in.shape[1]
    half = gate_in.shape[1] // 2
    n1, n2, n3 = rows // 2, rows // 4, rows // 8
    row, col = lax.axis_index("row"), lax.axis_index("col")
    core, y_hi, x = row % 2, (row // 2) % 2, row // 4
    y_lo, z = col // 4, col % 4
    bit_a, bit_b = x // 2, (x + x // 2) % 2
    flip_a, flip_b = 3 - x, x + 1 - 2 * (x % 2)
    keep1 = core * bit_a + (1 - core) * bit_b
    keep2 = core * bit_b + (1 - core) * bit_a
    x1 = core * flip_a + (1 - core) * flip_b
    x2 = core * flip_b + (1 - core) * flip_a
    sibling = (row + 1 - 2 * core, col)
    first = (x1 * 4 + y_hi * 2 + core, col)
    second = (x2 * 4 + y_hi * 2 + core, col)
    far = (x * 4 + (1 - y_hi) * 2 + core, col)
    k1 = keep1 * n1
    k2 = k1 + keep2 * n2
    k3 = k2 + y_hi * n3

    def at_col(step, sign):
        dy, dz = step // 4, step % 4
        return (row, (y_lo + dy - 2 * y_lo * dy) * 4 + (z + sign * dz + 4) % 4)

    def span(start, size):
        return pl.ds(pl.multiple_of(start, n3), size)

    def block(s):
        return pl.ds(pl.multiple_of(s * rows, rows), rows)

    def remote(step, s, m):
        if step == CORE:
            src, dst, dev = part.at[s, m, 1 - core], r_core.at[s, m], sibling
        elif step == FIRST:
            src, dst, dev = part.at[s, m, core, span((1 - keep1) * n1, n1)], r_first.at[s, m], first
        elif step == SECOND:
            src = part.at[s, m, core, span(k1 + (1 - keep2) * n2, n2)]
            dst, dev = r_second.at[s, m], second
        elif step == FAR:
            src = part.at[s, m, core, span(k2 + (1 - y_hi) * n3, n3)]
            dst, dev = r_far.at[s, m], far
        else:
            start, size, dev = {
                FAR_BACK: (k3, n3, far),
                SECOND_BACK: (k2, n2, second),
                FIRST_BACK: (k1, n1, first),
                CORE_BACK: (0, rows, sibling),
            }[step]
            src = dst = full.at[m, core, span(s * rows + start, size)]
        return pltpu.make_async_remote_copy(
            src_ref=src,
            dst_ref=dst,
            send_sem=send_sem.at[step, s, m],
            recv_sem=recv_sem.at[step, s, m],
            device_id=dev,
            device_id_type=MESH,
        )

    def column(which, s):
        ref = (xs, ys)[which]
        return pltpu.make_async_remote_copy(
            src_ref=ref.at[pl.ds(0, rows)],
            dst_ref=ref.at[block(s)],
            send_sem=col_send.at[which, s],
            recv_sem=col_recv.at[which, s],
            device_id=at_col(s, -1),
            device_id_type=MESH,
        )

    def dx_copy(s):
        return pltpu.make_async_remote_copy(
            src_ref=dx_send.at[s],
            dst_ref=dx_recv.at[s],
            send_sem=dx_ssem.at[s],
            recv_sem=dx_rsem.at[s],
            device_id=at_col(s, 1),
            device_id_type=MESH,
        )

    def load(i, src, dst):
        return pltpu.make_async_copy(src, dst, local_sem.at[i])

    loads = [
        load(0, x_in, xs.at[pl.ds(0, rows)]),
        load(1, y_in, ys.at[pl.ds(0, rows)]),
        load(2, gate_in, wg),
        load(3, up_in, wu),
        load(4, down_in, wd),
    ]
    for copy in loads:
        copy.start()

    barrier = pltpu.get_barrier_semaphore()
    partners = [sibling, first, second, far] + [at_col(s, 1) for s in range(1, BLOCKS)]
    for dev in partners:
        pl.semaphore_signal(barrier, inc=1, device_id=dev, device_id_type=MESH)
    pl.semaphore_wait(barrier, len(partners))

    loads[0].wait()
    loads[1].wait()
    for s in range(1, BLOCKS):
        column(0, s).start()
        column(1, s).start()
    for copy in loads[2:]:
        copy.wait()

    def f32(v):
        return v.astype(jnp.float32)

    def partials(s):
        @pl.when(s > 0)
        def _():
            column(0, s).wait_recv()
            column(1, s).wait_recv()

        for m in range(3):
            for h in range(2):
                if m < 2:
                    value = dot(xs[block(s), :], (wg, wu)[m][:, h * half : (h + 1) * half])
                else:
                    value = dot(ys[block(s), :], wd[h * half : (h + 1) * half, :], NT)
                part[s, m, h] = value.astype(jnp.bfloat16)
            remote(CORE, s, m).start()

    def send_first(s):
        for m in range(3):
            remote(CORE, s, m).wait_recv()
            q = span((1 - keep1) * n1, n1)
            total = f32(part[s, m, core, q, :]) + f32(r_core[s, m, q, :])
            part[s, m, core, q, :] = total.astype(jnp.bfloat16)
            remote(FIRST, s, m).start()

    def send_second(s):
        for m in range(3):
            remote(FIRST, s, m).wait_recv()
            o = (1 - keep2) * n2
            q = span(k1 + o, n2)
            total = (
                f32(part[s, m, core, q, :])
                + f32(r_core[s, m, q, :])
                + f32(r_first[s, m, span(o, n2), :])
            )
            part[s, m, core, q, :] = total.astype(jnp.bfloat16)
            remote(SECOND, s, m).start()

    def send_far(s):
        for m in range(3):
            remote(SECOND, s, m).wait_recv()
            o = (1 - y_hi) * n3
            q = span(k2 + o, n3)
            total = (
                f32(part[s, m, core, q, :])
                + f32(r_core[s, m, q, :])
                + f32(r_first[s, m, span(keep2 * n2 + o, n3), :])
                + f32(r_second[s, m, span(o, n3), :])
            )
            part[s, m, core, q, :] = total.astype(jnp.bfloat16)
            remote(FAR, s, m).start()

    def activate(s):
        q = span(k3, n3)
        sums = []
        for m in range(3):
            remote(FAR, s, m).wait_recv()
            total = (
                f32(part[s, m, core, q, :])
                + f32(r_core[s, m, q, :])
                + f32(r_first[s, m, span(keep2 * n2 + y_hi * n3, n3), :])
                + f32(r_second[s, m, span(y_hi * n3, n3), :])
                + f32(r_far[s, m])
            )
            sums.append(f32(total.astype(jnp.bfloat16)))
        gate, up, grad = sums
        sig = 1.0 / (1.0 + jnp.exp(-gate))
        act = gate * sig
        out = (act * up, grad * up * sig * (1.0 + gate * (1.0 - sig)), grad * act)
        for m in range(3):
            full[m, core, span(s * rows + k3, n3), :] = out[m].astype(jnp.bfloat16)
            remote(FAR_BACK, s, m).start()

    def forward(step, s):
        for m in range(3):
            remote(step - 1, s, m).wait_recv()
            remote(step, s, m).start()

    def input_grad(s):
        for m in range(3):
            remote(CORE_BACK, s, m).wait_recv()
        total = None
        for m, w in ((1, wg), (2, wu)):
            for h in range(2):
                term = dot(full[m, h, block(s), :], w[:, h * half : (h + 1) * half], NT)
                total = term if total is None else total + term
        value = total.astype(jnp.bfloat16)

        @pl.when(s == 0)
        def _():
            dx_recv[0] = value

        @pl.when(s > 0)
        def _():
            dx_send[s] = value
            dx_copy(s).start()

    def weight_grads(start, depth, opening, closing):
        tokens = pl.ds(start, depth)

        def put(acc, out, at, value):
            if not opening:
                value = value + acc[at]
            if closing:
                out[at] = value.astype(jnp.bfloat16)
            else:
                acc[at] = value

        tile = 128
        for m, acc, out in ((1, acc_gate, wg), (2, acc_up, wu)):
            for h in range(2):

                @pl.loop(0, width // tile)
                def _(i):
                    r = pl.ds(pl.multiple_of(i * tile, tile), tile)
                    value = dot(xs[tokens, r], full[m, h, tokens, :], TN)
                    put(acc, out, (r, slice(h * half, (h + 1) * half)), value)

        for h in range(2):

            @pl.loop(0, half // tile)
            def _(i):
                r = pl.ds(pl.multiple_of(i * tile, tile), tile)
                value = dot(full[0, h, tokens, r], ys[tokens, :], TN)
                put(acc_down, wd, (pl.ds(pl.multiple_of(h * half + i * tile, tile), tile), slice(None)), value)

    def on(t, delay, step):
        @pl.when((t >= delay) & (t < delay + BLOCKS))
        def _():
            step(t - delay)

    last = BLOCKS + 7

    @pl.loop(0, last + 1)
    def _(t):
        on(t, 2, send_second)
        on(t, 3, send_far)
        on(t, 4, activate)
        on(t, 5, lambda s: forward(SECOND_BACK, s))
        on(t, 6, lambda s: forward(FIRST_BACK, s))
        on(t, 7, lambda s: forward(CORE_BACK, s))
        on(t, 0, partials)
        on(t, 1, send_first)
        on(t, 8, input_grad)

        @pl.when(t == 8 + 3)
        def _():
            weight_grads(0, 4 * rows, True, False)

        @pl.when(t == 8 + 5)
        def _():
            weight_grads(4 * rows, 2 * rows, False, False)

    weight_grads(6 * rows, 2 * rows, False, True)
    stores = [load(0, wg, gg_out), load(1, wu, gu_out), load(2, wd, gd_out)]
    for copy in stores:
        copy.start()
    total = f32(dx_recv[0])
    for s in range(1, BLOCKS):
        dx_copy(s).wait_recv()
        total = total + f32(dx_recv[s])
    dx_out[...] = total.astype(jnp.bfloat16)
    store = load(3, dx_out, gx_out)
    store.start()

    @pl.loop(0, BLOCKS)
    def _(s):
        for step in range(STEPS):
            for m in range(3):
                remote(step, s, m).wait_send()

    for s in range(1, BLOCKS):
        column(0, s).wait_send()
        column(1, s).wait_send()
        dx_copy(s).wait_send()
    for copy in stores:
        copy.wait()
    store.wait()


def on_device(inputs, cotangent, gate_weight, up_weight, down_weight):
    rows, width = inputs.shape
    columns = gate_weight.shape[1]
    half, tokens = columns // 2, rows * BLOCKS
    bf16, f32 = jnp.bfloat16, jnp.float32
    anywhere = pl.BlockSpec(memory_space=pl.ANY)
    dma = pltpu.SemaphoreType.DMA
    return pl.pallas_call(
        kernel,
        out_shape=[
            jax.ShapeDtypeStruct(a.shape, bf16) for a in (inputs, gate_weight, up_weight, down_weight)
        ],
        in_specs=[anywhere] * 5,
        out_specs=[anywhere] * 4,
        scratch_shapes=[
            pltpu.VMEM((tokens, width), bf16),
            pltpu.VMEM((tokens, width), bf16),
            pltpu.VMEM((width, columns), bf16),
            pltpu.VMEM((width, columns), bf16),
            pltpu.VMEM((columns, width), bf16),
            pltpu.VMEM((BLOCKS, 3, 2, rows, half), bf16),
            pltpu.VMEM((BLOCKS, 3, rows, half), bf16),
            pltpu.VMEM((BLOCKS, 3, rows // 2, half), bf16),
            pltpu.VMEM((BLOCKS, 3, rows // 4, half), bf16),
            pltpu.VMEM((BLOCKS, 3, rows // 8, half), bf16),
            pltpu.VMEM((3, 2, tokens, half), bf16),
            pltpu.VMEM((width, columns), f32),
            pltpu.VMEM((width, columns), f32),
            pltpu.VMEM((columns, width), f32),
            pltpu.VMEM((BLOCKS, rows, width), bf16),
            pltpu.VMEM((BLOCKS, rows, width), bf16),
            pltpu.VMEM((rows, width), bf16),
            dma((5,)),
            dma((STEPS, BLOCKS, 3)),
            dma((STEPS, BLOCKS, 3)),
            dma((2, BLOCKS)),
            dma((2, BLOCKS)),
            dma((BLOCKS,)),
            dma((BLOCKS,)),
        ],
        compiler_params=pltpu.CompilerParams(
            collective_id=0, has_side_effects=True, vmem_limit_bytes=62 * 1024 * 1024
        ),
        cost_estimate=pl.CostEstimate(
            flops=16 * tokens * width * columns, bytes_accessed=24_000_000, transcendentals=0
        ),
    )(inputs, cotangent, gate_weight, up_weight, down_weight)


def solution(mesh):
    placed = (P("col", "row"), P("col", "row"), P("row", "col"), P("row", "col"), P("col", "row"))
    return jax.shard_map(
        on_device,
        mesh=mesh,
        in_specs=placed,
        out_specs=(P("col", "row"), P("row", "col"), P("row", "col"), P("col", "row")),
        check_vma=False,
    )
```

time: 502 us -> 184 us (0.37)
  waiting for transfers between devices: 398 us -> 0 us
  Pallas kernels: 0 us -> 172 us
  matrix products: 40.1 us -> 0 us
  local copies, waits for them, and re-layouts: 38.6 us -> 7.94 us
  between operations: 14.2 us -> 0.64 us
  other arithmetic: 5.64 us -> 0 us
    reduce_scatter x3 -> x0, waiting for transfers between devices: 244 us -> none  [the longest x2 229 us: reduce_rows(): lax.psum_scatter(product(panel).reshape(lax.axis_size('row') * share_rows...]
    pallas_call x0 -> x1, Pallas kernels: none -> 172 us  [on_device(): pl.pallas_call(kernel, out_shape=[jax.ShapeDtypeStruct(a.shape, bf16) for...]
    all_gather x4 -> x0, waiting for transfers between devices: 152 us -> none  [the longest x2 104 us: collect(): return lax.all_gather(pieces, 'row', axis=0, tiled=True)]
    dot_general x5 -> x0, matrix products: 40.1 us -> none  [the longest x1 11.5 us: forward_term(): return jnp.dot(rows_block, weights_pair, preferred_element_type=jnp.float32)]
    reshape x1 -> x0, local copies, waits for them, and re-layouts: 14.4 us -> none  [reduce_rows(): product(panel).reshape(lax.axis_size('row') * share_rows, stacked, columns)]
    all_gather x1 -> x0, local copies, waits for them, and re-layouts: 9.92 us -> none  [collect(): return lax.all_gather(pieces, 'row', axis=0, tiled=True)]
    unnamed x13 -> x8, local copies, waits for them, and re-layouts: 10.8 us -> 7.94 us
  transfers between devices with their start and end apart: 7 -> 0, of which waited for: 7 -> 0; matrix products, arithmetic and copies ran while one was open for 16% -> 0% of each run, Pallas kernels for 0% -> 0%
where the time goes in v1:
time: 184 us; the launch traced here: 181 us
  Pallas kernels  172 us (93%)
  local copies, waits for them, and re-layouts  7.94 us (4%)
    pallas_call x1, Pallas kernels, on_device(): pl.pallas_call(kernel, out_shape=[jax.ShapeDtypeStruct(a.shape, bf16) for...  172 us
    unnamed x8, local copies, waits for them, and re-layouts  7.94 us

profile of v1, /device:TPU:1, one launch (start us, length us, event | category | flops | bytes accessed | tf_op | source)
XLA Modules:
  0.0 180.8 jit_solution(14272003482637581292)
XLA Ops:
  0.6 172.3 %shard_map.84 = (bf16[128,512]{1,0:T(8,128)(2,1)}, bf16[512,1792]{1,0:T(8,128)(2,1)}, bf16[512,1792]{1,0:T(8,128)(2,1)}, bf16[1792,512]{1,0:T(8,128)(2,1)}) custom-call(bf16[128,512]{1,0:T(8,128)(2,1)} %x_in.1, bf16[128,512]{1,0:T(8,128)(2,1)} %y_in.1, bf16[512,1792]{1,0:T(8,128)(2,1)} %gate_in.1, bf16[512,1792]{1,0:T(8,128)(2,1)} %up_in.1, ...), custom_call_target="tpu_custom_call" | custom-call | flops 15032385536 | bytes 24000000 | tf_op jit(solution)/shard_map/pallas_call | solution.py:321
  172.9 1.6 copy.13
  174.5 0.0 copy-start.1
  174.5 3.0 %copy.14 = bf16[512,1792]{1,0:T(8,128)(2,1)} copy(bf16[512,1792]{1,0:T(8,128)(2,1)} %get-tuple-element.9) | data formatting | bytes 3670016
  177.4 0.0 copy-done.1
  177.5 0.0 copy-start
  177.5 1.2 copy.15
  178.7 0.9 copy-done
  179.6 1.2 copy.16
Async XLA Ops:
  174.5 3.0 %copy-start.1 = (bf16[512,1792]{1,0:T(8,128)(2,1)S(1)}, bf16[512,1792]{1,0:T(8,128)(2,1)}, u32[]{:S(2)}) copy-start(bf16[512,1792]{1,0:T(8,128)(2,1)} %get-tuple-element.10) | copy-start | bytes 5505028
  177.5 2.2 %copy-start = (bf16[1792,512]{1,0:T(8,128)(2,1)S(1)}, bf16[1792,512]{1,0:T(8,128)(2,1)}, u32[]{:S(2)}) copy-start(bf16[1792,512]{1,0:T(8,128)(2,1)} %get-tuple-element.11) | copy-start | bytes 5505028

commit v2 on v0

v2 whole, which is shorter than its diff:
```python
import jax
import jax.numpy as jnp
from jax import lax
from jax.experimental import pallas as pl
from jax.experimental.pallas import tpu as pltpu
from jax.sharding import PartitionSpec as P

MESH = pl.DeviceIdType.MESH
BLOCKS = 8
OFFSETS = ((0, 0), (0, 1), (1, 0), (0, 3), (1, 1), (1, 3), (0, 2), (1, 2))
SENDS = {1: (0, 1), 2: (0, 0), 3: (0, 3), 4: (2, 1), 5: (2, 3), 6: (0, 2), 7: (2, 2)}
SEND_AT = {1: (6,), 2: (4, 5), 3: (7,)}
DELAYS = (0, 1, 3, 5, 7, 9, 11, 14, 16)
ORDER = (1, 5, 8, 6, 3, 2, 0, 4, 7)
FAR_FIRST = (2,)
NT = (((1,), (1,)), ((), ()))
TN = (((0,), (0,)), ((), ()))


def dot(a, b, dims=(((1,), (0,)), ((), ()))):
    return lax.dot_general(a, b, dims, preferred_element_type=jnp.float32)


def exchange_kernel(
    x_in, y_in, gate_in, up_in, down_in,
    gx_out, x_out, y_out, full_out,
    xs, ys, wg, wu, wd, part, r_core, r_one, r_two, r_three, full,
    dx_send, dx_recv, dx_out, local_sem, send_sem, recv_sem, col_send, col_recv, dx_ssem, dx_rsem, out_sem,
):
    rows = x_in.shape[0]
    half = gate_in.shape[1] // 2
    shape = part.shape[3:]
    row, col = lax.axis_index("row"), lax.axis_index("col")
    core, y_hi, x = row % 2, (row // 2) % 2, row // 4
    y_lo, z = col // 4, col % 4
    bit_a, bit_b = x // 2, (x + x // 2) % 2
    flip_a, flip_b = 3 - x, x + 1 - 2 * (x % 2)
    i1 = core * bit_a + (1 - core) * bit_b
    i2 = core * bit_b + (1 - core) * bit_a
    i3 = y_hi
    x1 = core * flip_a + (1 - core) * flip_b
    x2 = core * flip_b + (1 - core) * flip_a
    sibling = (row + 1 - 2 * core, col)
    first = (x1 * 4 + y_hi * 2 + core, col)
    second = (x2 * 4 + y_hi * 2 + core, col)
    far = (x * 4 + (1 - y_hi) * 2 + core, col)
    every = slice(None)

    def at_col(k, sign):
        dy, dz = OFFSETS[k]
        return (row, (1 - y_lo if dy else y_lo) * 4 + (z + sign * dz + 4) % 4)

    def leaving(m):
        if m in FAR_FIRST:
            return (far, (every, every, 1 - i3)), (first, (1 - i1, every, i3)), (second, (i1, 1 - i2, i3))
        return (first, (1 - i1,)), (second, (i1, 1 - i2)), (far, (i1, i2, 1 - i3))

    def returning(m):
        if m in FAR_FIRST:
            return (second, (i1, i2, i3)), (first, (i1, every, i3)), (far, (every, every, i3))
        return (far, (i1, i2, i3)), (second, (i1, i2)), (first, (i1,))

    def kept(m):
        if m in FAR_FIRST:
            return ((1 - i1,),), ((i1, 1 - i2), (1 - i2,)), ((i1, i2), (i2,))
        return ((1 - i2,),), ((i2, 1 - i3), (1 - i3,)), ((i2, i3), (i3,))

    def remote(step, s, m):
        if step == 0:
            src, dst, dev = part.at[s, m, 1 - core], r_core.at[s, m], sibling
        elif step < 4:
            dev, place = leaving(m)[step - 1]
            src, dst = part.at[(s, m, core) + place], (r_one, r_two, r_three)[step - 1].at[s, m]
        else:
            dev, place = (sibling, ()) if step == 7 else returning(m)[step - 4]
            src = dst = full.at[(m, core, s) + place]
        return pltpu.make_async_remote_copy(
            src_ref=src,
            dst_ref=dst,
            send_sem=send_sem.at[step, s, m],
            recv_sem=recv_sem.at[step, s, m],
            device_id=dev,
            device_id_type=MESH,
        )

    def column(which, k, s=None):
        source, dz = SENDS.get(k, (0, 1))
        ref = (xs, ys)[which]
        target = at_col(k, -1) if source == 0 else (row, y_lo * 4 + (z - OFFSETS[k][1] + 4) % 4)
        slot = k if s is None else s
        return pltpu.make_async_remote_copy(
            src_ref=ref.at[pl.ds(source * rows, rows)],
            dst_ref=ref.at[pl.ds(pl.multiple_of(slot * rows, rows), rows)],
            send_sem=col_send.at[which, slot],
            recv_sem=col_recv.at[which, slot],
            device_id=target,
            device_id_type=MESH,
        )

    def dx_copy(k):
        return pltpu.make_async_remote_copy(
            src_ref=dx_send.at[k],
            dst_ref=dx_recv.at[k],
            send_sem=dx_ssem.at[k],
            recv_sem=dx_rsem.at[k],
            device_id=at_col(k, 1),
            device_id_type=MESH,
        )

    def local(i, src, dst):
        return pltpu.make_async_copy(src, dst, local_sem.at[i])

    def save(s, m, h):
        columns = slice(h * half, (h + 1) * half)
        return pltpu.make_async_copy(
            full.at[m, h, s], full_out.at[m, s, :, :, :, :, columns], out_sem.at[s, m, h]
        )

    loads = [
        local(0, x_in, xs.at[pl.ds(0, rows)]),
        local(1, y_in, ys.at[pl.ds(0, rows)]),
        local(2, gate_in, wg),
        local(3, up_in, wu),
        local(4, down_in, wd),
    ]
    for copy in loads:
        copy.start()

    barrier = pltpu.get_barrier_semaphore()
    partners = [sibling, first, second, far] + [at_col(k, 1) for k in range(1, BLOCKS)]
    for dev in partners:
        pl.semaphore_signal(barrier, inc=1, device_id=dev, device_id_type=MESH)
    pl.semaphore_wait(barrier, len(partners))

    for which in range(2):
        loads[which].wait()
        for k in (1, 2, 3):
            column(which, k).start()
    for copy in loads[2:]:
        copy.wait()

    def f32(v):
        return v.astype(jnp.float32)

    def gathered(which, s):
        @pl.when(s > 0)
        def _():
            column(which, 1, s).wait_recv()

        for at, ks in SEND_AT.items():

            @pl.when(s == at)
            def _():
                for k in ks:
                    column(which, k).start()

    def partials(s):
        block = pl.ds(pl.multiple_of(s * rows, rows), rows)
        for m in range(3):
            if m != 1:
                gathered(m // 2, s)
            for h in range(2):
                if m < 2:
                    value = dot(xs[block, :], (wg, wu)[m][:, h * half : (h + 1) * half])
                else:
                    value = dot(ys[block, :], wd[h * half : (h + 1) * half, :], NT)
                part[s, m, h] = value.astype(jnp.bfloat16).reshape(shape)
            remote(0, s, m).start()

    def reduce(step, s):
        for m in range(3):
            remote(step - 1, s, m).wait_recv()
            place = leaving(m)[step - 1][1]
            total = f32(part[(s, m, core) + place]) + f32(r_core[(s, m) + place])
            if step > 1:
                for ref, at in zip((r_one, r_two), kept(m)[step - 2]):
                    total = total + f32(ref[(s, m) + at])
            part[(s, m, core) + place] = total.astype(jnp.bfloat16)
            remote(step, s, m).start()

    def activate(s):
        sums = []
        for m in range(3):
            remote(3, s, m).wait_recv()
            total = f32(part[s, m, core, i1, i2, i3]) + f32(r_core[s, m, i1, i2, i3])
            for ref, at in zip((r_one, r_two), kept(m)[2]):
                total = total + f32(ref[(s, m) + at])
            total = total + f32(r_three[s, m])
            sums.append(f32(total.astype(jnp.bfloat16)))
        gate, up, grad = sums
        sig = 1.0 / (1.0 + jnp.exp(-gate))
        act = gate * sig
        out = (act * up, grad * up * sig * (1.0 + gate * (1.0 - sig)), grad * act)
        for m in range(3):
            full[m, core, s, i1, i2, i3] = out[m].astype(jnp.bfloat16)
            remote(4, s, m).start()

    def spread(step, s):
        for m in range(3):
            remote(step - 1, s, m).wait_recv()
            remote(step, s, m).start()

    def input_grad(s):
        for m in range(3):
            remote(7, s, m).wait_recv()
            for h in range(2):
                save(s, m, h).start()
        total = None
        for m, w in ((1, wg), (2, wu)):
            for h in range(2):
                values = full[m, h, s].reshape(rows, half)
                term = dot(values, w[:, h * half : (h + 1) * half], NT)
                total = term if total is None else total + term
        value = total.astype(jnp.bfloat16)

        @pl.when(s == 0)
        def _():
            dx_recv[0] = value

        @pl.when(s > 0)
        def _():
            dx_send[s] = value

        for k in range(1, BLOCKS):

            @pl.when(s == k)
            def _():
                dx_copy(k).start()

    def stage(number, s):
        if number == 0:
            partials(s)
        elif number < 4:
            reduce(number, s)
        elif number == 4:
            activate(s)
        elif number < 8:
            spread(number, s)
        else:
            input_grad(s)

    @pl.loop(0, BLOCKS + max(DELAYS))
    def _(t):
        for number in ORDER:
            delay = DELAYS[number]

            @pl.when((t >= delay) & (t < delay + BLOCKS))
            def _():
                stage(number, t - delay)

    stores = [local(0, xs, x_out), local(1, ys, y_out)]
    for copy in stores:
        copy.start()
    total = f32(dx_recv[0])
    for k in range(1, BLOCKS):
        dx_copy(k).wait_recv()
        total = total + f32(dx_recv[k])
    dx_out[...] = total.astype(jnp.bfloat16)
    stores.append(local(2, dx_out, gx_out))
    stores[-1].start()

    @pl.loop(0, BLOCKS)
    def _(s):
        for m in range(3):
            for step in range(8):
                remote(step, s, m).wait_send()
            for h in range(2):
                save(s, m, h).wait()

    for k in range(1, BLOCKS):
        column(0, k).wait_send()
        column(1, k).wait_send()
        dx_copy(k).wait_send()
    for copy in stores:
        copy.wait()


def weights_kernel(gx_in, x_ref, y_ref, full_ref, gx_out, gate_out, up_out, down_out):
    step = pl.program_id(0)
    values = full_ref[0]

    @pl.when(step == 0)
    def _():
        gx_out[...] = gx_in[...]

    for at, out in ((0, gate_out), (2, up_out)):

        @pl.when((step >= at) & (step < at + 2))
        def _():
            out[...] = dot(x_ref[...], values, TN).astype(jnp.bfloat16)

    @pl.when(step >= 4)
    def _():
        down_out[...] = dot(values, y_ref[...], TN).astype(jnp.bfloat16)


def on_device(inputs, cotangent, gate_weight, up_weight, down_weight):
    rows, width = inputs.shape
    columns = gate_weight.shape[1]
    half, tokens = columns // 2, rows * BLOCKS
    bf16 = jnp.bfloat16
    block = (2, 2, 2, rows // 8)
    anywhere = pl.BlockSpec(memory_space=pl.ANY)
    dma = pltpu.SemaphoreType.DMA
    gx, x_all, y_all, full = pl.pallas_call(
        exchange_kernel,
        out_shape=[
            jax.ShapeDtypeStruct((rows, width), bf16),
            jax.ShapeDtypeStruct((tokens, width), bf16),
            jax.ShapeDtypeStruct((tokens, width), bf16),
            jax.ShapeDtypeStruct((3, BLOCKS, *block, columns), bf16),
        ],
        in_specs=[anywhere] * 5,
        out_specs=[anywhere] * 4,
        scratch_shapes=[
            pltpu.VMEM((tokens, width), bf16),
            pltpu.VMEM((tokens, width), bf16),
            pltpu.VMEM((width, columns), bf16),
            pltpu.VMEM((width, columns), bf16),
            pltpu.VMEM((columns, width), bf16),
            pltpu.VMEM((BLOCKS, 3, 2, *block, half), bf16),
            pltpu.VMEM((BLOCKS, 3, *block, half), bf16),
            pltpu.VMEM((BLOCKS, 3, *block[1:], half), bf16),
            pltpu.VMEM((BLOCKS, 3, *block[2:], half), bf16),
            pltpu.VMEM((BLOCKS, 3, *block[3:], half), bf16),
            pltpu.VMEM((3, 2, BLOCKS, *block, half), bf16),
            pltpu.VMEM((BLOCKS, rows, width), bf16),
            pltpu.VMEM((BLOCKS, rows, width), bf16),
            pltpu.VMEM((rows, width), bf16),
            dma((5,)),
            dma((8, BLOCKS, 3)),
            dma((8, BLOCKS, 3)),
            dma((2, BLOCKS)),
            dma((2, BLOCKS)),
            dma((BLOCKS,)),
            dma((BLOCKS,)),
            dma((BLOCKS, 3, 2)),
        ],
        compiler_params=pltpu.CompilerParams(
            collective_id=0, has_side_effects=True, vmem_limit_bytes=56 * 1024 * 1024
        ),
        cost_estimate=pl.CostEstimate(
            flops=10 * tokens * width * columns, bytes_accessed=24_000_000, transcendentals=0
        ),
    )(inputs, cotangent, gate_weight, up_weight, down_weight)

    def whole(shape):
        return pl.BlockSpec(shape, lambda j: (0, 0))

    return pl.pallas_call(
        weights_kernel,
        grid=(6,),
        out_shape=[
            jax.ShapeDtypeStruct(a.shape, bf16) for a in (inputs, gate_weight, up_weight, down_weight)
        ],
        in_specs=[
            whole((rows, width)),
            whole((tokens, width)),
            whole((tokens, width)),
            pl.BlockSpec((1, tokens, half), lambda j: ((j // 2 + 1) % 3, 0, j % 2)),
        ],
        out_specs=[
            whole((rows, width)),
            pl.BlockSpec((width, half), lambda j: (0, jnp.minimum(j, 1))),
            pl.BlockSpec((width, half), lambda j: (0, jnp.clip(j - 2, 0, 1))),
            pl.BlockSpec((half, width), lambda j: (jnp.maximum(j - 4, 0), 0)),
        ],
        compiler_params=pltpu.CompilerParams(vmem_limit_bytes=56 * 1024 * 1024),
        cost_estimate=pl.CostEstimate(
            flops=6 * tokens * width * columns, bytes_accessed=20_000_000, transcendentals=0
        ),
    )(gx, x_all, y_all, full.reshape(3, tokens, columns))


def solution(mesh):
    placed = (P("col", "row"), P("col", "row"), P("row", "col"), P("row", "col"), P("col", "row"))
    return jax.shard_map(
        on_device,
        mesh=mesh,
        in_specs=placed,
        out_specs=(P("col", "row"), P("row", "col"), P("row", "col"), P("col", "row")),
        check_vma=False,
    )
```

time: 502 us -> 120 us (0.24)
  waiting for transfers between devices: 398 us -> 0 us
  Pallas kernels: 0 us -> 119 us
  matrix products: 40.1 us -> 0 us
  local copies, waits for them, and re-layouts: 38.6 us -> 0 us
  between operations: 14.2 us -> 0.64 us
  other arithmetic: 5.64 us -> 0 us
    reduce_scatter x3 -> x0, waiting for transfers between devices: 244 us -> none  [the longest x2 229 us: reduce_rows(): lax.psum_scatter(product(panel).reshape(lax.axis_size('row') * share_rows...]
    all_gather x4 -> x0, waiting for transfers between devices: 152 us -> none  [the longest x2 104 us: collect(): return lax.all_gather(pieces, 'row', axis=0, tiled=True)]
    pallas_call x0 -> x2, Pallas kernels: none -> 119 us  [the longest x1 106 us: on_device(): pl.pallas_call(exchange_kernel, out_shape=[jax.ShapeDtypeStruct((rows, wi...]
    dot_general x5 -> x0, matrix products: 40.1 us -> none  [the longest x1 11.5 us: forward_term(): return jnp.dot(rows_block, weights_pair, preferred_element_type=jnp.float32)]
    reshape x1 -> x0, local copies, waits for them, and re-layouts: 14.4 us -> none  [reduce_rows(): product(panel).reshape(lax.axis_size('row') * share_rows, stacked, columns)]
    unnamed x13 -> x0, local copies, waits for them, and re-layouts: 10.8 us -> none
    all_gather x1 -> x0, local copies, waits for them, and re-layouts: 9.92 us -> none  [collect(): return lax.all_gather(pieces, 'row', axis=0, tiled=True)]
  transfers between devices with their start and end apart: 7 -> 0, of which waited for: 7 -> 0; matrix products, arithmetic and copies ran while one was open for 16% -> 0% of each run, Pallas kernels for 0% -> 0%
where the time goes in v2:
time: 120 us; the launch traced here: 119 us
  Pallas kernels  119 us (99%)
    pallas_call x1, Pallas kernels, on_device(): pl.pallas_call(exchange_kernel, out_shape=[jax.ShapeDtypeStruct((rows, wi...  106 us
    pallas_call x1, Pallas kernels, on_device(): pl.pallas_call(weights_kernel, grid=(6,), out_shape=[jax.ShapeDtypeStruct...  13 us

profile of v2, /device:TPU:1, one launch (start us, length us, event | category | flops | bytes accessed | tf_op | source)
XLA Modules:
  0.0 119.4 jit_solution(12211442511865429488)
XLA Ops:
  0.6 105.8 %shard_map.84 = (bf16[128,512]{1,0:T(8,128)(2,1)}, bf16[1024,512]{1,0:T(8,128)(2,1)}, bf16[1024,512]{1,0:T(8,128)(2,1)}, bf16[3,8,2,2,2,16,1792]{6,5,4,3,2,1,0:T(8,128)(2,1)}) custom-call(bf16[128,512]{1,0:T(8,128)(2,1)} %x_in.1, bf16[128,512]{1,0:T(8,128)(2,1)} %y_in.1, bf16[512,1792]{1,0:T(8,128)(2,1)} %gate_in.1, bf16[512,1792]{1,0:T(8,128)(2,1)} %up_in.1, ...), custom_call_target="tpu_custom_call" | custom-call | flops 9395240960 | bytes 24000000 | tf_op jit(solution)/shard_map/pallas_call | solution.py:305
  106.4 13.0 %shard_map.85 = (bf16[128,512]{1,0:T(8,128)(2,1)}, bf16[512,1792]{1,0:T(8,128)(2,1)}, bf16[512,1792]{1,0:T(8,128)(2,1)}, bf16[1792,512]{1,0:T(8,128)(2,1)}) custom-call(bf16[128,512]{1,0:T(8,128)(2,1)} %get-tuple-element.8.gx_in, bf16[1024,512]{1,0:T(8,128)(2,1)} %get-tuple-element.9.x_ref, bf16[1024,512]{1,0:T(8,128)(2,1)} %get-tuple-element.10.y_ref, ...), custom_call_target="tpu_custom_call" | custom-call | flops 5637144576 | bytes 20000000 | tf_op jit(solution)/shard_map/pallas_call | solution.py:350

commit v3 on v2

v3 whole, which is shorter than its diff:
```python
import itertools

import jax
import jax.numpy as jnp
from jax import lax
from jax.experimental import pallas as pl
from jax.experimental.pallas import tpu as pltpu
from jax.sharding import PartitionSpec as P

MESH = pl.DeviceIdType.MESH
BLOCKS = 8
OFFSETS = ((0, 0), (0, 1), (1, 0), (0, 3), (1, 1), (1, 3), (0, 2), (1, 2))
SENDS = {1: (0, 1), 2: (0, 0), 3: (0, 3), 4: (2, 1), 5: (2, 3), 6: (0, 2), 7: (2, 2)}
SEND_AT = {1: (4, 5), 2: (6,), 3: (7,)}
DELAYS = (0, 1, 4, 6, 9, 10, 13, 15, 16, 16)
ORDER = ((4, 0), (2, 0), (2, 1), (2, 2), (6, 0), (6, 1), (6, 2), (3, 0), (3, 1), (3, 2), (1, 0), (1, 1), (1, 2), (8, 0), (7, 0), (7, 1), (7, 2), (9, 0), (9, 1), (9, 2), (5, 0), (5, 1), (5, 2), (0, 0), (0, 1), (0, 2))
FAR_FIRST = (2,)
FAR_LAST = (2,)
NT = (((1,), (1,)), ((), ()))
TN = (((0,), (0,)), ((), ()))


def dot(a, b, dims=(((1,), (0,)), ((), ()))):
    return lax.dot_general(a, b, dims, preferred_element_type=jnp.float32)


def exchange_kernel(
    x_in, y_in, gate_in, up_in, down_in,
    gx_out, gate_out, up_out, down_out,
    xs, ys, wg, wu, wd, part, r_core, r_one, r_two, r_three, full, acc_gate, acc_up, acc_down,
    dx_send, dx_recv, local_sem, send_sem, recv_sem, col_send, col_recv, dx_ssem, dx_rsem,
):
    rows, width = x_in.shape
    half = gate_in.shape[1] // 2
    shape = part.shape[3:]
    row, col = lax.axis_index("row"), lax.axis_index("col")
    core, y_hi, x = row % 2, (row // 2) % 2, row // 4
    y_lo, z = col // 4, col % 4
    bit_a, bit_b = x // 2, (x + x // 2) % 2
    flip_a, flip_b = 3 - x, x + 1 - 2 * (x % 2)
    i1 = core * bit_a + (1 - core) * bit_b
    i2 = core * bit_b + (1 - core) * bit_a
    i3 = y_hi
    x1 = core * flip_a + (1 - core) * flip_b
    x2 = core * flip_b + (1 - core) * flip_a
    sibling = (row + 1 - 2 * core, col)
    first = (x1 * 4 + y_hi * 2 + core, col)
    second = (x2 * 4 + y_hi * 2 + core, col)
    far = (x * 4 + (1 - y_hi) * 2 + core, col)
    every = slice(None)

    def at_col(k, sign):
        dy, dz = OFFSETS[k]
        return (row, (1 - y_lo if dy else y_lo) * 4 + (z + sign * dz + 4) % 4)

    def leaving(m):
        if m in FAR_FIRST:
            return (far, (every, every, 1 - i3)), (first, (1 - i1, every, i3)), (second, (i1, 1 - i2, i3))
        return (first, (1 - i1,)), (second, (i1, 1 - i2)), (far, (i1, i2, 1 - i3))

    def returning(m):
        if m in FAR_LAST:
            return (second, (i1, i2, i3)), (first, (i1, every, i3)), (far, (every, every, i3))
        return (far, (i1, i2, i3)), (second, (i1, i2)), (first, (i1,))

    def kept(m):
        if m in FAR_FIRST:
            return ((1 - i1,),), ((i1, 1 - i2), (1 - i2,)), ((i1, i2), (i2,))
        return ((1 - i2,),), ((i2, 1 - i3), (1 - i3,)), ((i2, i3), (i3,))

    def remote(step, s, m):
        if step == 0:
            src, dst, dev = part.at[s, m, 1 - core], r_core.at[s, m], sibling
        elif step < 4:
            dev, place = leaving(m)[step - 1]
            src, dst = part.at[(s, m, core) + place], (r_one, r_two, r_three)[step - 1].at[s, m]
        else:
            dev, place = (sibling, ()) if step == 7 else returning(m)[step - 4]
            src = dst = full.at[(m, core, s) + place]
        return pltpu.make_async_remote_copy(
            src_ref=src,
            dst_ref=dst,
            send_sem=send_sem.at[step, s, m],
            recv_sem=recv_sem.at[step, s, m],
            device_id=dev,
            device_id_type=MESH,
        )

    def column(which, k, s=None):
        source, dz = SENDS.get(k, (0, 1))
        ref = (xs, ys)[which]
        target = at_col(k, -1) if source == 0 else (row, y_lo * 4 + (z - OFFSETS[k][1] + 4) % 4)
        slot = k if s is None else s
        return pltpu.make_async_remote_copy(
            src_ref=ref.at[pl.ds(source * rows, rows)],
            dst_ref=ref.at[pl.ds(pl.multiple_of(slot * rows, rows), rows)],
            send_sem=col_send.at[which, slot],
            recv_sem=col_recv.at[which, slot],
            device_id=target,
            device_id_type=MESH,
        )

    def dx_copy(k):
        return pltpu.make_async_remote_copy(
            src_ref=dx_send.at[k],
            dst_ref=dx_recv.at[k],
            send_sem=dx_ssem.at[k],
            recv_sem=dx_rsem.at[k],
            device_id=at_col(k, 1),
            device_id_type=MESH,
        )

    def local(i, src, dst):
        return pltpu.make_async_copy(src, dst, local_sem.at[i])

    def f32(v):
        return v.astype(jnp.float32)

    def gathered(which, s):
        @pl.when(s != 2)
        def _():
            column(which, 1, s).wait_recv()

        @pl.when(s == 1)
        def _():
            column(which, 1, 2).wait_recv()

        for at, ks in SEND_AT.items():

            @pl.when(s == at)
            def _():
                for k in ks:
                    column(which, k).start()

    def multiply(s, m):
        block = pl.ds(s * rows if isinstance(s, int) else pl.multiple_of(s * rows, rows), rows)
        for h in range(2):
            if m < 2:
                value = dot(xs[block, :], (wg, wu)[m][:, h * half : (h + 1) * half])
            else:
                value = dot(ys[block, :], wd[h * half : (h + 1) * half, :], NT)
            part[s, m, h] = value.astype(jnp.bfloat16).reshape(shape)

    def partials(s, m):
        if m != 1:
            gathered(m // 2, s)
        multiply(s, m)
        remote(0, s, m).start()

    def reduce(step, s, m):
        remote(step - 1, s, m).wait_recv()
        place = leaving(m)[step - 1][1]
        total = f32(part[(s, m, core) + place]) + f32(r_core[(s, m) + place])
        if step > 1:
            for ref, at in zip((r_one, r_two), kept(m)[step - 2]):
                total = total + f32(ref[(s, m) + at])
        part[(s, m, core) + place] = total.astype(jnp.bfloat16)
        remote(step, s, m).start()

    def activate(j):
        s = (j + 1) % BLOCKS
        sums = []
        for m in range(3):
            remote(3, s, m).wait_recv()
            total = f32(part[s, m, core, i1, i2, i3]) + f32(r_core[s, m, i1, i2, i3])
            for ref, at in zip((r_one, r_two), kept(m)[2]):
                total = total + f32(ref[(s, m) + at])
            total = total + f32(r_three[s, m])
            sums.append(f32(total.astype(jnp.bfloat16)))
        gate, up, grad = sums
        sig = 1.0 / (1.0 + jnp.exp(-gate))
        act = gate * sig
        out = (act * up, grad * up * sig * (1.0 + gate * (1.0 - sig)), grad * act)
        for m in range(3):
            full[m, core, j, i1, i2, i3] = out[m].astype(jnp.bfloat16)
            remote(4, j, m).start()

    def spread(step, j, m):
        remote(step - 1, j, m).wait_recv()
        remote(step, j, m).start()

    def input_grad(j):
        for m in range(3):
            remote(7, j, m).wait_recv()
        total = None
        for m, w in ((1, wg), (2, wu)):
            for h in range(2):
                values = full[m, h, j].reshape(rows, half)
                term = dot(values, w[:, h * half : (h + 1) * half], NT)
                total = term if total is None else total + term
        value = total.astype(jnp.bfloat16)

        @pl.when(j == BLOCKS - 1)
        def _():
            dx_recv[0] = value

        @pl.when(j < BLOCKS - 1)
        def _():
            dx_send[j + 1] = value

        for k in range(1, BLOCKS):

            @pl.when(j == k - 1)
            def _():
                dx_copy(k).start()

    def weight_part(p, q, closing=False):
        m, h = (1, 2, 0)[q // 2], q % 2
        pair = pl.ds(2 * p, 2)
        start = (2 * p + 1) * rows
        tokens = pl.ds(start if closing else pl.multiple_of(start, rows), 2 * rows)

        def put(acc, out, at, value):
            value = value + acc[at]
            if closing:
                out[at] = value.astype(jnp.bfloat16)
            else:
                acc[at] = value

        if m:
            acc, out = ((acc_gate, gate_out), (acc_up, up_out))[m - 1]
            values = full[m, h, pair].reshape(2 * rows, half)
            tile = 256
            for i in range(width // tile):
                r = slice(i * tile, (i + 1) * tile)
                put(acc, out, (r, slice(h * half, (h + 1) * half)), dot(xs[tokens, r], values, TN))
        else:
            tile = 128

            @pl.loop(0, half // tile)
            def _(i):
                r = pl.ds(pl.multiple_of(i * tile, tile), tile)
                values = full[0, h, pair, :, :, :, :, r].reshape(2 * rows, tile)
                at = pl.ds(pl.multiple_of(h * half + i * tile, tile), tile)
                put(acc_down, down_out, (at, slice(None)), dot(values, ys[tokens, :], TN))

    def weight_parts(j, i):
        @pl.when((j % 2 == 1) & (j < BLOCKS - 1))
        def _():
            weight_part(j // 2, i)

        @pl.when((j % 2 == 0) & (j > 0))
        def _():
            weight_part(j // 2 - 1, 3 + i)

    def work(stage, j, m):
        if stage == 0:
            partials(j, m)
        elif stage < 4:
            reduce(stage, j, m)
        elif stage == 4:
            activate(j)
        elif stage < 8:
            spread(stage, j, m)
        elif stage == 8:
            input_grad(j)
        else:
            weight_parts(j, m)

    loads = [
        local(0, x_in, xs.at[pl.ds(0, rows)]),
        local(1, y_in, ys.at[pl.ds(0, rows)]),
        local(5, x_in, xs.at[pl.ds(BLOCKS * rows, rows)]),
        local(6, y_in, ys.at[pl.ds(BLOCKS * rows, rows)]),
        local(2, gate_in, wg),
        local(3, up_in, wu),
        local(4, down_in, wd),
    ]
    for copy in loads:
        copy.start()

    barrier = pltpu.get_barrier_semaphore()
    partners = [sibling, first, second, far] + [at_col(k, 1) for k in range(1, BLOCKS)]
    for dev in partners:
        pl.semaphore_signal(barrier, inc=1, device_id=dev, device_id_type=MESH)
    for acc in (acc_gate, acc_up, acc_down):
        acc[...] = jnp.zeros_like(acc)
    loads[0].wait()
    loads[1].wait()
    pl.semaphore_wait(barrier, len(partners))
    for which in range(2):
        for k in (1, 2, 3):
            column(which, k).start()
    for copy in loads[2:]:
        copy.wait()
    for m in range(3):
        multiply(0, m)
        remote(0, 0, m).start()

    @pl.loop(0, BLOCKS + max(DELAYS))
    def _(t):
        for stage, items in itertools.groupby(ORDER, lambda item: item[0]):
            delay = DELAYS[stage]

            @pl.when((t >= delay + (stage == 0)) & (t < delay + BLOCKS))
            def _():
                for _, m in items:
                    work(stage, t - delay, m)

    for q in range(6):
        weight_part(BLOCKS // 2 - 1, q, True)
    total = f32(dx_recv[0])
    for k in range(1, BLOCKS):
        dx_copy(k).wait_recv()
        total = total + f32(dx_recv[k])
    gx_out[...] = total.astype(jnp.bfloat16)

    @pl.loop(0, BLOCKS)
    def _(s):
        for m in range(3):
            for step in range(8):
                remote(step, s, m).wait_send()

    for k in range(1, BLOCKS):
        column(0, k).wait_send()
        column(1, k).wait_send()
        dx_copy(k).wait_send()


def place_kernel(*refs):
    sem = refs[-1]
    count = len(refs) // 2
    copies = [pltpu.make_async_copy(refs[i], refs[count + i], sem.at[i]) for i in range(count)]
    for copy in copies:
        copy.start()
    for copy in copies:
        copy.wait()


def on_device(inputs, cotangent, gate_weight, up_weight, down_weight):
    rows, width = inputs.shape
    columns = gate_weight.shape[1]
    half, tokens = columns // 2, rows * BLOCKS
    bf16 = jnp.bfloat16
    block = (2, 2, 2, rows // 8)
    anywhere = pl.BlockSpec(memory_space=pl.ANY)
    inside = pl.BlockSpec(memory_space=pltpu.VMEM)
    dma = pltpu.SemaphoreType.DMA
    results = [jax.ShapeDtypeStruct(a.shape, bf16) for a in (inputs, gate_weight, up_weight, down_weight)]
    grads = pl.pallas_call(
        exchange_kernel,
        out_shape=[pltpu.VMEM(a.shape, bf16) for a in results],
        in_specs=[anywhere] * 5,
        out_specs=[inside] * 4,
        scratch_shapes=[
            pltpu.VMEM((tokens + rows, width), bf16),
            pltpu.VMEM((tokens + rows, width), bf16),
            pltpu.VMEM((width, columns), bf16),
            pltpu.VMEM((width, columns), bf16),
            pltpu.VMEM((columns, width), bf16),
            pltpu.VMEM((BLOCKS, 3, 2, *block, half), bf16),
            pltpu.VMEM((BLOCKS, 3, *block, half), bf16),
            pltpu.VMEM((BLOCKS, 3, *block[1:], half), bf16),
            pltpu.VMEM((BLOCKS, 3, *block[2:], half), bf16),
            pltpu.VMEM((BLOCKS, 3, *block[3:], half), bf16),
            pltpu.VMEM((3, 2, BLOCKS, *block, half), bf16),
            pltpu.VMEM((width, columns), jnp.float32),
            pltpu.VMEM((width, columns), jnp.float32),
            pltpu.VMEM((columns, width), jnp.float32),
            pltpu.VMEM((BLOCKS, rows, width), bf16),
            pltpu.VMEM((BLOCKS, rows, width), bf16),
            dma((7,)),
            dma((8, BLOCKS, 3)),
            dma((8, BLOCKS, 3)),
            dma((2, BLOCKS)),
            dma((2, BLOCKS)),
            dma((BLOCKS,)),
            dma((BLOCKS,)),
        ],
        compiler_params=pltpu.CompilerParams(
            collective_id=0, has_side_effects=True, vmem_limit_bytes=56 * 1024 * 1024
        ),
        cost_estimate=pl.CostEstimate(
            flops=16 * tokens * width * columns, bytes_accessed=24_000_000, transcendentals=0
        ),
    )(inputs, cotangent, gate_weight, up_weight, down_weight)

    return pl.pallas_call(
        place_kernel,
        out_shape=results,
        in_specs=[inside] * 4,
        out_specs=[anywhere] * 4,
        scratch_shapes=[dma((4,))],
        compiler_params=pltpu.CompilerParams(vmem_limit_bytes=1024 * 1024),
        cost_estimate=pl.CostEstimate(flops=0, bytes_accessed=12_000_000, transcendentals=0),
    )(*grads)


def solution(mesh):
    placed = (P("col", "row"), P("col", "row"), P("row", "col"), P("row", "col"), P("col", "row"))
    return jax.shard_map(
        on_device,
        mesh=mesh,
        in_specs=placed,
        out_specs=(P("col", "row"), P("row", "col"), P("row", "col"), P("col", "row")),
        check_vma=False,
    )
```

time: 120 us -> 112 us (0.933)
  Pallas kernels: 119 us -> 111 us
    pallas_call x2, Pallas kernels: 119 us -> 111 us  [the longest x1 109 us: on_device(): pl.pallas_call(exchange_kernel, out_shape=[pltpu.VMEM(a.shape, bf16) for...]
where the time goes in v3:
time: 112 us
  Pallas kernels  111 us (99%)
    pallas_call x1, Pallas kernels, on_device(): pl.pallas_call(exchange_kernel, out_shape=[pltpu.VMEM(a.shape, bf16) for...  109 us
    pallas_call x1, Pallas kernels, on_device(): pl.pallas_call(place_kernel, out_shape=results, in_specs=[inside] * 4, ou...  2.52 us

profile of v3, /device:TPU:1, one launch (start us, length us, event | category | flops | bytes accessed | tf_op | source)
XLA Modules:
  0.0 112.0 jit_solution(2604004973081948138)
XLA Ops:
  0.6 108.8 %shard_map.84 = (bf16[128,512]{1,0:T(8,128)(2,1)S(1)}, bf16[512,1792]{1,0:T(8,128)(2,1)S(1)}, bf16[512,1792]{1,0:T(8,128)(2,1)S(1)}, bf16[1792,512]{1,0:T(8,128)(2,1)S(1)}) custom-call(bf16[128,512]{1,0:T(8,128)(2,1)} %x_in.1, bf16[128,512]{1,0:T(8,128)(2,1)} %y_in.1, bf16[512,1792]{1,0:T(8,128)(2,1)} %gate_in.1, bf16[512,1792]{1,0:T(8,128)(2,1)} %up_in.1, ...), custom_call_target="tpu_custom_call" | custom-call | flops 15032385536 | bytes 24000000 | tf_op jit(solution)/shard_map/pallas_call | solution.py:340
  109.5 2.5 %shard_map.85 = (bf16[128,512]{1,0:T(8,128)(2,1)}, bf16[512,1792]{1,0:T(8,128)(2,1)}, bf16[512,1792]{1,0:T(8,128)(2,1)}, bf16[1792,512]{1,0:T(8,128)(2,1)}) custom-call(bf16[128,512]{1,0:T(8,128)(2,1)S(1)} %get-tuple-element.8.refs_0_, bf16[512,1792]{1,0:T(8,128)(2,1)S(1)} %get-tuple-element.9.refs_1_, bf16[512,1792]{1,0:T(8,128)(2,1)S(1)} %get-tuple-element.10.refs_2_, ...), custom_call_target="tpu_custom_call" | custom-call | bytes 12000000 | tf_op jit(solution)/shard_map/pallas_call | solution.py:378

commit v4 on v3

--- a/solution.py
+++ b/solution.py
@@ -12,10 +12,11 @@
 OFFSETS = ((0, 0), (0, 1), (1, 0), (0, 3), (1, 1), (1, 3), (0, 2), (1, 2))
 SENDS = {1: (0, 1), 2: (0, 0), 3: (0, 3), 4: (2, 1), 5: (2, 3), 6: (0, 2), 7: (2, 2)}
 SEND_AT = {1: (4, 5), 2: (6,), 3: (7,)}
-DELAYS = (0, 1, 4, 6, 9, 10, 13, 15, 16, 16)
-ORDER = ((4, 0), (2, 0), (2, 1), (2, 2), (6, 0), (6, 1), (6, 2), (3, 0), (3, 1), (3, 2), (1, 0), (1, 1), (1, 2), (8, 0), (7, 0), (7, 1), (7, 2), (9, 0), (9, 1), (9, 2), (5, 0), (5, 1), (5, 2), (0, 0), (0, 1), (0, 2))
-FAR_FIRST = (2,)
-FAR_LAST = (2,)
+DELAYS = (0, 1, 3, 5, 8, 9, 12, 14, 15, 15)
+ORDER = ((4, 0), (2, 0), (2, 1), (6, 0), (6, 1), (3, 0), (3, 1), (1, 0), (1, 1), (8, 0), (7, 0), (7, 1), (9, 0), (9, 1), (9, 2), (5, 0), (5, 1), (0, 0), (0, 1))
+UNITS = (slice(0, 2), slice(2, 3))
+FAR_FIRST = (1,)
+FAR_LAST = (1,)
 NT = (((1,), (1,)), ((), ()))
 TN = (((0,), (0,)), ((), ()))
 
@@ -53,35 +54,36 @@
         dy, dz = OFFSETS[k]
         return (row, (1 - y_lo if dy else y_lo) * 4 + (z + sign * dz + 4) % 4)
 
-    def leaving(m):
-        if m in FAR_FIRST:
+    def leaving(u):
+        if u in FAR_FIRST:
             return (far, (every, every, 1 - i3)), (first, (1 - i1, every, i3)), (second, (i1, 1 - i2, i3))
         return (first, (1 - i1,)), (second, (i1, 1 - i2)), (far, (i1, i2, 1 - i3))
 
-    def returning(m):
-        if m in FAR_LAST:
+    def returning(u):
+        if u in FAR_LAST:
             return (second, (i1, i2, i3)), (first, (i1, every, i3)), (far, (every, every, i3))
         return (far, (i1, i2, i3)), (second, (i1, i2)), (first, (i1,))
 
-    def kept(m):
-        if m in FAR_FIRST:
+    def kept(u):
+        if u in FAR_FIRST:
             return ((1 - i1,),), ((i1, 1 - i2), (1 - i2,)), ((i1, i2), (i2,))
         return ((1 - i2,),), ((i2, 1 - i3), (1 - i3,)), ((i2, i3), (i3,))
 
-    def remote(step, s, m):
+    def remote(step, s, u):
+        ms = UNITS[u]
         if step == 0:
-            src, dst, dev = part.at[s, m, 1 - core], r_core.at[s, m], sibling
+            src, dst, dev = part.at[s, ms, 1 - core], r_core.at[s, ms], sibling
         elif step < 4:
-            dev, place = leaving(m)[step - 1]
-            src, dst = part.at[(s, m, core) + place], (r_one, r_two, r_three)[step - 1].at[s, m]
+            dev, place = leaving(u)[step - 1]
+            src, dst = part.at[(s, ms, core) + place], (r_one, r_two, r_three)[step - 1].at[s, ms]
         else:
-            dev, place = (sibling, ()) if step == 7 else returning(m)[step - 4]
-            src = dst = full.at[(m, core, s) + place]
+            dev, place = (sibling, ()) if step == 7 else returning(u)[step - 4]
+            src = dst = full.at[(ms, core, s) + place]
         return pltpu.make_async_remote_copy(
             src_ref=src,
             dst_ref=dst,
-            send_sem=send_sem.at[step, s, m],
-            recv_sem=recv_sem.at[step, s, m],
+            send_sem=send_sem.at[step, s, u],
+            recv_sem=recv_sem.at[step, s, u],
             device_id=dev,
             device_id_type=MESH,
         )
@@ -141,47 +143,49 @@
                 value = dot(ys[block, :], wd[h * half : (h + 1) * half, :], NT)
             part[s, m, h] = value.astype(jnp.bfloat16).reshape(shape)
 
-    def partials(s, m):
-        if m != 1:
-            gathered(m // 2, s)
-        multiply(s, m)
-        remote(0, s, m).start()
-
-    def reduce(step, s, m):
-        remote(step - 1, s, m).wait_recv()
-        place = leaving(m)[step - 1][1]
-        total = f32(part[(s, m, core) + place]) + f32(r_core[(s, m) + place])
+    def partials(s, u):
+        gathered(u, s)
+        for m in range(UNITS[u].start, UNITS[u].stop):
+            multiply(s, m)
+        remote(0, s, u).start()
+
+    def reduce(step, s, u):
+        remote(step - 1, s, u).wait_recv()
+        ms, place = UNITS[u], leaving(u)[step - 1][1]
+        total = f32(part[(s, ms, core) + place]) + f32(r_core[(s, ms) + place])
         if step > 1:
-            for ref, at in zip((r_one, r_two), kept(m)[step - 2]):
-                total = total + f32(ref[(s, m) + at])
-        part[(s, m, core) + place] = total.astype(jnp.bfloat16)
-        remote(step, s, m).start()
+            for ref, at in zip((r_one, r_two), kept(u)[step - 2]):
+                total = total + f32(ref[(s, ms) + at])
+        part[(s, ms, core) + place] = total.astype(jnp.bfloat16)
+        remote(step, s, u).start()
 
     def activate(j):
         s = (j + 1) % BLOCKS
         sums = []
-        for m in range(3):
-            remote(3, s, m).wait_recv()
-            total = f32(part[s, m, core, i1, i2, i3]) + f32(r_core[s, m, i1, i2, i3])
-            for ref, at in zip((r_one, r_two), kept(m)[2]):
-                total = total + f32(ref[(s, m) + at])
-            total = total + f32(r_three[s, m])
-            sums.append(f32(total.astype(jnp.bfloat16)))
+        for u, ms in enumerate(UNITS):
+            remote(3, s, u).wait_recv()
+            for m in range(ms.start, ms.stop):
+                total = f32(part[s, m, core, i1, i2, i3]) + f32(r_core[s, m, i1, i2, i3])
+                for ref, at in zip((r_one, r_two), kept(u)[2]):
+                    total = total + f32(ref[(s, m) + at])
+                total = total + f32(r_three[s, m])
+                sums.append(f32(total.astype(jnp.bfloat16)))
         gate, up, grad = sums
         sig = 1.0 / (1.0 + jnp.exp(-gate))
         act = gate * sig
         out = (act * up, grad * up * sig * (1.0 + gate * (1.0 - sig)), grad * act)
-        for m in range(3):
-            full[m, core, j, i1, i2, i3] = out[m].astype(jnp.bfloat16)
-            remote(4, j, m).start()
-
-    def spread(step, j, m):
-        remote(step - 1, j, m).wait_recv()
-        remote(step, j, m).start()
+        for u, ms in enumerate(UNITS):
+            for m in range(ms.start, ms.stop):
+                full[m, core, j, i1, i2, i3] = out[m].astype(jnp.bfloat16)
+            remote(4, j, u).start()
+
+    def spread(step, j, u):
+        remote(step - 1, j, u).wait_recv()
+        remote(step, j, u).start()
 
     def input_grad(j):
-        for m in range(3):
-            remote(7, j, m).wait_recv()
+        for u in range(len(UNITS)):
+            remote(7, j, u).wait_recv()
         total = None
         for m, w in ((1, wg), (2, wu)):
             for h in range(2):
@@ -283,9 +287,10 @@
             column(which, k).start()
     for copy in loads[2:]:
         copy.wait()
-    for m in range(3):
-        multiply(0, m)
-        remote(0, 0, m).start()
+    for u, ms in enumerate(UNITS):
+        for m in range(ms.start, ms.stop):
+            multiply(0, m)
+        remote(0, 0, u).start()
 
     @pl.loop(0, BLOCKS + max(DELAYS))
     def _(t):
@@ -307,9 +312,9 @@
 
     @pl.loop(0, BLOCKS)
     def _(s):
-        for m in range(3):
+        for u in range(len(UNITS)):
             for step in range(8):
-                remote(step, s, m).wait_send()
+                remote(step, s, u).wait_send()
 
     for k in range(1, BLOCKS):
         column(0, k).wait_send()
@@ -360,8 +365,8 @@
             pltpu.VMEM((BLOCKS, rows, width), bf16),
             pltpu.VMEM((BLOCKS, rows, width), bf16),
             dma((7,)),
-            dma((8, BLOCKS, 3)),
-            dma((8, BLOCKS, 3)),
+            dma((8, BLOCKS, 2)),
+            dma((8, BLOCKS, 2)),
             dma((2, BLOCKS)),
             dma((2, BLOCKS)),
             dma((BLOCKS,)),

time: 112 us -> 111 us (level)
    pallas_call x1, Pallas kernels: 109 us -> 107 us  [on_device(): pl.pallas_call(exchange_kernel, out_shape=[pltpu.VMEM(a.shape, bf16) for...]
where the time goes in v4:
time: 111 us
  Pallas kernels  110 us (99%)
    pallas_call x1, Pallas kernels, on_device(): pl.pallas_call(exchange_kernel, out_shape=[pltpu.VMEM(a.shape, bf16) for...  107 us
    pallas_call x1, Pallas kernels, on_device(): pl.pallas_call(place_kernel, out_shape=results, in_specs=[inside] * 4, ou...  2.52 us

profile of v4, /device:TPU:1, one launch (start us, length us, event | category | flops | bytes accessed | tf_op | source)
XLA Modules:
  0.0 110.6 jit_solution(16066953043704940400)
XLA Ops:
  0.6 107.4 %shard_map.84 = (bf16[128,512]{1,0:T(8,128)(2,1)S(1)}, bf16[512,1792]{1,0:T(8,128)(2,1)S(1)}, bf16[512,1792]{1,0:T(8,128)(2,1)S(1)}, bf16[1792,512]{1,0:T(8,128)(2,1)S(1)}) custom-call(bf16[128,512]{1,0:T(8,128)(2,1)} %x_in.1, bf16[128,512]{1,0:T(8,128)(2,1)} %y_in.1, bf16[512,1792]{1,0:T(8,128)(2,1)} %gate_in.1, bf16[512,1792]{1,0:T(8,128)(2,1)} %up_in.1, ...), custom_call_target="tpu_custom_call" | custom-call | flops 15032385536 | bytes 24000000 | tf_op jit(solution)/shard_map/pallas_call | solution.py:345
  108.1 2.5 %shard_map.85 = (bf16[128,512]{1,0:T(8,128)(2,1)}, bf16[512,1792]{1,0:T(8,128)(2,1)}, bf16[512,1792]{1,0:T(8,128)(2,1)}, bf16[1792,512]{1,0:T(8,128)(2,1)}) custom-call(bf16[128,512]{1,0:T(8,128)(2,1)S(1)} %get-tuple-element.8.refs_0_, bf16[512,1792]{1,0:T(8,128)(2,1)S(1)} %get-tuple-element.9.refs_1_, bf16[512,1792]{1,0:T(8,128)(2,1)S(1)} %get-tuple-element.10.refs_2_, ...), custom_call_target="tpu_custom_call" | custom-call | bytes 12000000 | tf_op jit(solution)/shard_map/pallas_call | solution.py:383

commit v5 on v4

--- a/solution.py
+++ b/solution.py
@@ -183,7 +183,15 @@
         remote(step - 1, j, u).wait_recv()
         remote(step, j, u).start()
 
+    def close(h):
+        for q in (0, 2, 4):
+            weight_part(BLOCKS // 2 - 1, q, True, h)
+
     def input_grad(j):
+        @pl.when(j == BLOCKS - 1)
+        def _():
+            close(core)
+
         for u in range(len(UNITS)):
             remote(7, j, u).wait_recv()
         total = None
@@ -208,8 +216,9 @@
             def _():
                 dx_copy(k).start()
 
-    def weight_part(p, q, closing=False):
-        m, h = (1, 2, 0)[q // 2], q % 2
+    def weight_part(p, q, closing=False, h=None):
+        m, h = (1, 2, 0)[q // 2], q % 2 if h is None else h
+        here = pl.ds(h * half if isinstance(h, int) else pl.multiple_of(h * half, 128), half)
         pair = pl.ds(2 * p, 2)
         start = (2 * p + 1) * rows
         tokens = pl.ds(start if closing else pl.multiple_of(start, rows), 2 * rows)
@@ -227,7 +236,7 @@
             tile = 256
             for i in range(width // tile):
                 r = slice(i * tile, (i + 1) * tile)
-                put(acc, out, (r, slice(h * half, (h + 1) * half)), dot(xs[tokens, r], values, TN))
+                put(acc, out, (r, here), dot(xs[tokens, r], values, TN))
         else:
             tile = 128
 
@@ -302,8 +311,7 @@
                 for _, m in items:
                     work(stage, t - delay, m)
 
-    for q in range(6):
-        weight_part(BLOCKS // 2 - 1, q, True)
+    close(1 - core)
     total = f32(dx_recv[0])
     for k in range(1, BLOCKS):
         dx_copy(k).wait_recv()

time: 111 us -> 111 us (level)
  no operation moved by 1% of the time
where the time goes in v5:
time: 111 us
  Pallas kernels  110 us (99%)
    pallas_call x1, Pallas kernels, on_device(): pl.pallas_call(exchange_kernel, out_shape=[pltpu.VMEM(a.shape, bf16) for...  108 us
    pallas_call x1, Pallas kernels, on_device(): pl.pallas_call(place_kernel, out_shape=results, in_specs=[inside] * 4, ou...  2.52 us

profile of v5, /device:TPU:1, one launch (start us, length us, event | category | flops | bytes accessed | tf_op | source)
XLA Modules:
  0.0 110.9 jit_solution(4563041938679385063)
XLA Ops:
  0.6 107.7 %shard_map.84 = (bf16[128,512]{1,0:T(8,128)(2,1)S(1)}, bf16[512,1792]{1,0:T(8,128)(2,1)S(1)}, bf16[512,1792]{1,0:T(8,128)(2,1)S(1)}, bf16[1792,512]{1,0:T(8,128)(2,1)S(1)}) custom-call(bf16[128,512]{1,0:T(8,128)(2,1)} %x_in.1, bf16[128,512]{1,0:T(8,128)(2,1)} %y_in.1, bf16[512,1792]{1,0:T(8,128)(2,1)} %gate_in.1, bf16[512,1792]{1,0:T(8,128)(2,1)} %up_in.1, ...), custom_call_target="tpu_custom_call" | custom-call | flops 15032385536 | bytes 24000000 | tf_op jit(solution)/shard_map/pallas_call | solution.py:353
  108.3 2.5 %shard_map.85 = (bf16[128,512]{1,0:T(8,128)(2,1)}, bf16[512,1792]{1,0:T(8,128)(2,1)}, bf16[512,1792]{1,0:T(8,128)(2,1)}, bf16[1792,512]{1,0:T(8,128)(2,1)}) custom-call(bf16[128,512]{1,0:T(8,128)(2,1)S(1)} %get-tuple-element.8.refs_0_, bf16[512,1792]{1,0:T(8,128)(2,1)S(1)} %get-tuple-element.9.refs_1_, bf16[512,1792]{1,0:T(8,128)(2,1)S(1)} %get-tuple-element.10.refs_2_, ...), custom_call_target="tpu_custom_call" | custom-call | bytes 12000000 | tf_op jit(solution)/shard_map/pallas_call | solution.py:391
